TPU v7x, 32 devices: a whole 2x2x4 slice. The times are simulated.
32 devices in a mesh: dp: 8 (over z, x), expert: 4 (over y, core).
Axes of the slice: x: 2, y: 2, z: 4, core: 2. Of those that a mesh axis runs over, the one named last changes fastest.
Arguments:
- saved_inputs: bfloat16 [8, 4, 1024, 4096], P('dp', 'expert'), may hold values from -6 to 6
- saved_grads: bfloat16 [8, 4, 1024, 1536], P('dp', 'expert'), may hold values from -6 to 6
- row_counts: int32 [8, 4], P('dp', 'expert'), may hold values from 1 to 1024, as said below
- row_seq: int32 [8, 4, 1024], P('dp', 'expert'), may hold values from 0 to 255
- proj_in: bfloat16 [4096, 32], replicated, may hold values from -0.09375 to 0.09375
- proj_out: bfloat16 [1536, 32], replicated, may hold values from -0.15625 to 0.15625
Outputs:
- logged: bfloat16 [4, 2048, 1024], P(None, ('dp', 'expert'))
- fisher: float32 [1024, 4, 1024], P('dp', 'expert')
Inputs may be any that keep to these rules, and one draw needn't show every extreme that they name: Slots from row_counts on are padding with arbitrary contents; row_counts reaches 1024 for some expert in every draw.
All inputs are finite; a program needn't handle non-finite values.
Results may differ from a plain program's by a relative error of at most 0.012.
Values may be sent and summed in bfloat16 or wider, within the bound.
A program may use at most 64 MiB of HBM per device.

v0:
```python
import functools

import jax
import jax.numpy as jnp
from jax import lax
from jax.experimental import pallas as pl
from jax.experimental.pallas import tpu as pltpu
from jax.sharding import PartitionSpec as P

SEQ_DEV = 256
CHUNKS = 4
PIECES = 2
MESH = pl.DeviceIdType.MESH
NT = (((1,), (1,)), ((), ()))


def kernel(
    n_dp,
    n_exp,
    lo,
    count_ref,
    seq_ref,
    x_hbm,
    g_hbm,
    pin_hbm,
    pout_hbm,
    logged_ref,
    fisher_ref,
    xb,
    gb,
    pin,
    pout,
    wide_in,
    wide_out,
    fac,
    seqs,
    outer,
    onehot,
    gt,
    lg,
    acc,
    give,
    got,
    lives,
    in_sem,
    p_sem,
    send_sem,
    recv_sem,
    lsend_sem,
    lrecv_sem,
    xsend_sem,
    xrecv_sem,
    local_sem,
):
    hi = n_dp // lo
    msgs = CHUNKS + 1
    rank = pin_hbm.shape[0]
    cap = x_hbm.shape[0]
    rows = cap // CHUNKS
    lanes = seq_ref.shape[1]
    share = SEQ_DEV // n_exp
    fb = acc.shape[0] // lo

    dp = lax.axis_index("dp")
    ex = lax.axis_index("expert")
    z = dp // lo
    x = dp % lo

    p_copies = [
        pltpu.make_async_copy(pin_hbm, pin, p_sem.at[0]),
        pltpu.make_async_copy(pout_hbm, pout, p_sem.at[1]),
    ]
    for c in p_copies:
        c.start()

    def load(ch):
        at = pl.ds(ch * rows, rows)
        return (
            pltpu.make_async_copy(x_hbm.at[at], xb.at[at], in_sem.at[2 * ch]),
            pltpu.make_async_copy(g_hbm.at[at], gb.at[at], in_sem.at[2 * ch + 1]),
        )

    for ch in range(CHUNKS):
        for c in load(ch):
            c.start()

    barrier = pltpu.get_barrier_semaphore()

    def greet(device):
        pl.semaphore_signal(barrier, inc=1, device_id=device, device_id_type=MESH)

    for s in range(1, lo):
        greet((z * lo + lax.rem(x + s, lo), ex))
    for s in range(1, n_exp):
        greet((dp, lax.rem(ex + s, n_exp)))

    @pl.when(z > 0)
    def _():
        greet((dp - lo, ex))

    @pl.when(z < hi - 1)
    def _():
        greet((dp + lo, ex))

    def copy_of(blk, m, way, device):
        ref = seqs.at[blk] if m == 0 else fac.at[blk * CHUNKS + (m - 1)]
        return pltpu.make_async_remote_copy(
            src_ref=ref,
            dst_ref=ref,
            send_sem=send_sem.at[(way * hi + blk) * msgs + m],
            recv_sem=recv_sem.at[blk * msgs + m],
            device_id=(device, ex),
            device_id_type=MESH,
        )

    def send_on(sz, m, act):
        @pl.when((sz <= z) & (z < hi - 1))
        def _():
            act(copy_of(sz, m, 0, dp + lo))

        @pl.when((sz >= z) & (z > 0))
        def _():
            act(copy_of(sz, m, 1, dp - lo))

    start = lambda c: c.start()

    def recv(blk, m):
        copy_of(blk, m, 0, dp).wait_recv()

    slot = (
        lax.broadcasted_iota(jnp.int32, seq_ref.shape, 0) * lanes
        + lax.broadcasted_iota(jnp.int32, seq_ref.shape, 1)
    )
    seqs[z] = jnp.where(slot < count_ref[0, 0], seq_ref[...], -1)

    for c in p_copies:
        c.wait()
    for src, dst, before in ((pin, wide_in, 0), (pout, wide_out, rank)):
        blank = lambda r: [jnp.zeros((r, src.shape[1]), jnp.float32)] if r else []
        tall = blank(before) + [src[...].astype(jnp.float32)] + blank(lanes - rank - before)
        dst[...] = jnp.concatenate(tall, axis=0).T.astype(jnp.bfloat16)
    for ch in range(CHUNKS):
        for c in load(ch):
            c.wait()
        at = pl.ds(ch * rows, rows)
        both = jnp.dot(xb[at], wide_in[...], preferred_element_type=jnp.float32)
        both += jnp.dot(gb[at], wide_out[...], preferred_element_type=jnp.float32)
        fac[z * CHUNKS + ch] = both.T[: 2 * rank].astype(jnp.bfloat16)
        if ch == 0:
            greeted = (lo - 1) + (n_exp - 1) + jnp.where(z > 0, 1, 0) + jnp.where(z < hi - 1, 1, 0)
            pl.semaphore_wait(barrier, greeted)
            send_on(z, 0, start)
        send_on(z, ch + 1, start)

    def build(blk):
        for ch in range(CHUNKS):
            at = pl.ds(ch * rows, rows)
            f = fac[blk * CHUNKS + ch]
            wide = f[rank:].astype(jnp.float32)
            for k in range(rank):
                row = jnp.broadcast_to(wide[k : k + 1], (16, rows)).astype(jnp.bfloat16)
                for h in range(0, rank, 16):
                    outer[k * rank + h : k * rank + h + 16, at] = row * f[h : h + 16]
        ids = seqs[blk]
        want = lax.broadcasted_iota(jnp.int32, (SEQ_DEV, lanes), 0)
        for c in range(cap // lanes):
            onehot[:, c * lanes : (c + 1) * lanes] = jnp.where(
                want == ids[c : c + 1], 1.0, 0.0
            ).astype(jnp.bfloat16)

    def gram():
        gt[...] = lax.dot_general(
            outer[...], onehot[...], NT, preferred_element_type=jnp.float32
        ).astype(jnp.bfloat16)
        mine = gt[pl.ds(pl.multiple_of(z * lo * fb, lo * fb), lo * fb), :]
        return lax.dot_general(mine, gt[...], NT, preferred_element_type=jnp.float32)

    build(z)
    lg[...] = lax.dot_general(
        onehot[...], outer[...], NT, preferred_element_type=jnp.float32
    ).astype(jnp.bfloat16)

    def rows_of(e):
        return lg.at[pl.ds(pl.multiple_of(e * share, share), share)]

    def log_copy(s):
        to = lax.rem(ex + s, n_exp)
        return pltpu.make_async_remote_copy(
            src_ref=rows_of(to),
            dst_ref=logged_ref.at[ex],
            send_sem=lsend_sem.at[s - 1],
            recv_sem=lrecv_sem.at[s - 1],
            device_id=(dp, to),
            device_id_type=MESH,
        )

    def receive(d):
        for m in range(msgs):
            for side in (-1, 1):
                sz = z + side * d

                @pl.when((sz >= 0) & (sz < hi))
                def _():
                    recv(sz, m)
                    send_on(sz, m, start)

    for s in range(1, n_exp):
        log_copy(s).start()
    keep = pltpu.make_async_copy(rows_of(ex), logged_ref.at[ex], local_sem)
    keep.start()
    receive(1)
    acc[...] = gram()

    def at_distance(d, carry):
        receive(d + 1)

        def one(side, carry):
            sz = z + d * (2 * side - 1)

            @pl.when((sz >= 0) & (sz < hi))
            def _():
                build(sz)
                acc[...] += gram()

            return carry

        return lax.fori_loop(0, 2, one, carry)

    lax.fori_loop(1, hi, at_distance, 0)

    live = jnp.zeros(seq_ref.shape, jnp.float32)
    for p in range(hi):
        live += jnp.where(seqs[p] >= 0, 1.0, 0.0)
    lives[0] = live

    piece = fb // PIECES

    def rows_at(q):
        return pl.ds(q * piece, piece)

    def across(s, q):
        to = z * lo + lax.rem(x + s, lo)
        k = (s - 1) * (PIECES + 1) + q + 1
        src, dst = (lives.at[0], lives.at[s]) if q < 0 else (
            give.at[s, rows_at(q)],
            got.at[s, rows_at(q)],
        )
        return pltpu.make_async_remote_copy(
            src_ref=src,
            dst_ref=dst,
            send_sem=xsend_sem.at[k],
            recv_sem=xrecv_sem.at[k],
            device_id=(to, ex),
            device_id_type=MESH,
        )

    for s in range(1, lo):
        across(s, -1).start()
        theirs = lax.rem(x + s, lo) * fb
        for q in range(PIECES):
            at = pl.ds(pl.multiple_of(theirs + q * piece, piece), piece)
            give[s, rows_at(q)] = acc[at].astype(jnp.bfloat16)
            across(s, q).start()
    for s in range(1, lo):
        across(s, -1).wait_recv()
        live += lives[s]
    scale = 1.0 / jnp.sum(live)
    tiles = acc.shape[1] // lanes
    for q in range(PIECES):
        at = pl.ds(pl.multiple_of(x * fb + q * piece, piece), piece)
        total = acc[at]
        for s in range(1, lo):
            across(s, q).wait_recv()
            total += got[s, rows_at(q)].astype(jnp.float32)
        total *= scale
        for c in range(tiles):
            fisher_ref[pl.ds(q * piece * tiles + c, piece, stride=tiles), :] = total[
                :, c * lanes : (c + 1) * lanes
            ]

    def drain(sz, carry):
        for m in range(msgs):
            send_on(sz, m, lambda c: c.wait_send())
        return carry

    lax.fori_loop(0, hi, drain, 0)
    for s in range(1, lo):
        for q in range(-1, PIECES):
            across(s, q).wait_send()
    keep.wait()
    for s in range(1, n_exp):
        log_copy(s).wait()


def place_kernel(pieces, *refs):
    in_sems, out_sems = refs[-2:]
    n = (len(refs) - 2) // 3
    loads, stores = [], []
    for src, dst, held in zip(refs[:n], refs[n : 2 * n], refs[2 * n : 3 * n]):
        step = src.shape[0] // pieces
        for i in range(pieces):
            at = pl.ds(i * step, step)
            k = len(loads)
            loads.append(pltpu.make_async_copy(src.at[at], held.at[at], in_sems.at[k]))
            stores.append(pltpu.make_async_copy(held.at[at], dst.at[at], out_sems.at[k]))
    for c in loads:
        c.start()
    for c, d in zip(loads, stores):
        c.wait()
        d.start()
    for d in stores:
        d.wait()


def place(*arrays):
    pieces = 4
    hbm = pl.BlockSpec(memory_space=pl.ANY)
    return pl.pallas_call(
        functools.partial(place_kernel, pieces),
        out_shape=tuple(jax.ShapeDtypeStruct(a.shape, a.dtype) for a in arrays),
        in_specs=[hbm] * len(arrays),
        out_specs=(hbm,) * len(arrays),
        scratch_shapes=[pltpu.VMEM(a.shape, a.dtype) for a in arrays]
        + [pltpu.SemaphoreType.DMA((pieces * len(arrays),))] * 2,
        compiler_params=pltpu.CompilerParams(vmem_limit_bytes=60 * 1024 * 1024),
        name="place",
    )(*arrays)


def body(n_dp, n_exp, saved_inputs, saved_grads, row_counts, row_seq, proj_in, proj_out):
    cap, width = saved_inputs.shape[2:]
    ff = saved_grads.shape[3]
    rank = proj_in.shape[1]
    square = rank * rank
    lanes = 128
    lo = 2 if n_dp % 2 == 0 else 1
    hi = n_dp // lo
    share = SEQ_DEV // n_exp
    rows = cap // CHUNKS
    msgs = CHUNKS + 1
    vmem = pl.BlockSpec(memory_space=pltpu.VMEM)
    hbm = pl.BlockSpec(memory_space=pl.ANY)
    logged, fisher = pl.pallas_call(
        functools.partial(kernel, n_dp, n_exp, lo),
        out_shape=(
            jax.ShapeDtypeStruct((n_exp, share, square), jnp.bfloat16),
            jax.ShapeDtypeStruct((square // n_dp * square // lanes, lanes), jnp.float32),
        ),
        in_specs=[pl.BlockSpec(memory_space=pltpu.SMEM), vmem, hbm, hbm, hbm, hbm],
        out_specs=(hbm, vmem),
        scratch_shapes=[
            pltpu.VMEM((cap, width), jnp.bfloat16),
            pltpu.VMEM((cap, ff), jnp.bfloat16),
            pltpu.VMEM((rank, width), jnp.bfloat16),
            pltpu.VMEM((rank, ff), jnp.bfloat16),
            pltpu.VMEM((width, lanes), jnp.bfloat16),
            pltpu.VMEM((ff, lanes), jnp.bfloat16),
            pltpu.VMEM((hi * CHUNKS, 2 * rank, rows), jnp.bfloat16),
            pltpu.VMEM((hi, cap // lanes, lanes), jnp.int32),
            pltpu.VMEM((square, cap), jnp.bfloat16),
            pltpu.VMEM((SEQ_DEV, cap), jnp.bfloat16),
            pltpu.VMEM((square, SEQ_DEV), jnp.bfloat16),
            pltpu.VMEM((SEQ_DEV, square), jnp.bfloat16),
            pltpu.VMEM((square // hi, square), jnp.float32),
            pltpu.VMEM((lo, square // n_dp, square), jnp.bfloat16),
            pltpu.VMEM((lo, square // n_dp, square), jnp.bfloat16),
            pltpu.VMEM((lo, cap // lanes, lanes), jnp.float32),
            pltpu.SemaphoreType.DMA((2 * CHUNKS,)),
            pltpu.SemaphoreType.DMA((2,)),
            pltpu.SemaphoreType.DMA((2 * hi * msgs,)),
            pltpu.SemaphoreType.DMA((hi * msgs,)),
            pltpu.SemaphoreType.DMA((n_exp - 1,)),
            pltpu.SemaphoreType.DMA((n_exp - 1,)),
            pltpu.SemaphoreType.DMA((max(lo - 1, 1) * (PIECES + 1),)),
            pltpu.SemaphoreType.DMA((max(lo - 1, 1) * (PIECES + 1),)),
            pltpu.SemaphoreType.DMA,
        ],
        compiler_params=pltpu.CompilerParams(
            collective_id=0, has_side_effects=True, vmem_limit_bytes=56 * 1024 * 1024
        ),
    )(
        row_counts,
        row_seq.reshape(cap // lanes, lanes),
        saved_inputs.reshape(cap, width),
        saved_grads.reshape(cap, ff),
        proj_in.T,
        proj_out.T,
    )
    logged, fisher = place(logged, fisher)
    return logged, fisher.reshape(square // n_dp, 1, square)


def solution(mesh):
    in_specs = (
        P("dp", "expert", None, None),
        P("dp", "expert", None, None),
        P("dp", "expert"),
        P("dp", "expert", None),
        P(),
        P(),
    )
    out_specs = (P(None, ("dp", "expert"), None), P("dp", "expert", None))
    return jax.shard_map(
        functools.partial(body, mesh.shape["dp"], mesh.shape["expert"]),
        mesh=mesh,
        in_specs=in_specs,
        out_specs=out_specs,
        check_vma=False,
    )
```

profile of v0, /device:TPU:0, one launch (start us, length us, event | category | flops | bytes accessed | tf_op | source)
XLA Modules:
  0.0 35.6 jit_solution(15939705937279835850)
XLA Ops:
  1.3 32.3 %shard_map.77 = (bf16[4,64,1024]{2,1,0:T(8,128)(2,1)}, f32[1024,128]{1,0:T(8,128)}) custom-call(s32[1,1]{1,0:T(1,128)S(6)} %copy.9.count_ref, s32[8,128]{1,0:T(8,128)} %bitcast.10, bf16[1024,4096]{1,0:T(8,128)(2,1)} %bitcast.6, bf16[1024,1536]{1,0:T(8,128)(2,1)} %bitcast.7, bf16[32,4096]{1,0:T(8,128)(2,1)} %bitcast.8, bf16[32,1536]{1,0:T(8,128)(2,1)} %bitcast.9), custom_call_target="tpu_custom_call" | custom-call | tf_op jit(solution)/shard_map/pallas_call | solution.py:343
  33.6 2.1 %place.1 = (bf16[4,64,1024]{2,1,0:T(8,128)(2,1)}, f32[1024,128]{1,0:T(8,128)}) custom-call(bf16[4,64,1024]{2,1,0:T(8,128)(2,1)} %get-tuple-element.6.refs_0_, f32[1024,128]{1,0:T(8,128)} %get-tuple-element.7.refs_1_), custom_call_target="tpu_custom_call" | custom-call | tf_op jit(solution)/shard_map/place/pallas_call | solution.py:318
where the time goes:
time: 35.8 us; the launch traced here: 35.6 us
  Pallas kernels  34.4 us (96%)
  between operations  1.28 us (4%)
    pallas_call x1, Pallas kernels, body(): pl.pallas_call(functools.partial(kernel, n_dp, n_exp, lo), out_shape=(jax...  32.3 us
    pallas_call x1, Pallas kernels, place(): pl.pallas_call(functools.partial(place_kernel, pieces), out_shape=tuple((...  2.09 us

commit v1 on v0

--- a/solution.py
+++ b/solution.py
@@ -9,6 +9,7 @@
 
 SEQ_DEV = 256
 CHUNKS = 4
+AHEAD = 2
 PIECES = 2
 MESH = pl.DeviceIdType.MESH
 NT = (((1,), (1,)), ((), ()))
@@ -80,7 +81,7 @@
             pltpu.make_async_copy(g_hbm.at[at], gb.at[at], in_sem.at[2 * ch + 1]),
         )
 
-    for ch in range(CHUNKS):
+    for ch in range(AHEAD):
         for c in load(ch):
             c.start()
 
@@ -94,38 +95,23 @@
     for s in range(1, n_exp):
         greet((dp, lax.rem(ex + s, n_exp)))
 
-    @pl.when(z > 0)
-    def _():
-        greet((dp - lo, ex))
-
-    @pl.when(z < hi - 1)
-    def _():
-        greet((dp + lo, ex))
-
-    def copy_of(blk, m, way, device):
-        ref = seqs.at[blk] if m == 0 else fac.at[blk * CHUNKS + (m - 1)]
+    for s in range(1, hi):
+        greet((lax.rem(z + s, hi) * lo + x, ex))
+
+    def copy_of(src, m, s):
+        ref = seqs.at[src] if m == 0 else fac.at[src * CHUNKS + (m - 1)]
         return pltpu.make_async_remote_copy(
             src_ref=ref,
             dst_ref=ref,
-            send_sem=send_sem.at[(way * hi + blk) * msgs + m],
-            recv_sem=recv_sem.at[blk * msgs + m],
-            device_id=(device, ex),
+            send_sem=send_sem.at[(s - 1) * msgs + m],
+            recv_sem=recv_sem.at[src * msgs + m],
+            device_id=(lax.rem(z + s, hi) * lo + x, ex),
             device_id_type=MESH,
         )
 
-    def send_on(sz, m, act):
-        @pl.when((sz <= z) & (z < hi - 1))
-        def _():
-            act(copy_of(sz, m, 0, dp + lo))
-
-        @pl.when((sz >= z) & (z > 0))
-        def _():
-            act(copy_of(sz, m, 1, dp - lo))
-
-    start = lambda c: c.start()
-
-    def recv(blk, m):
-        copy_of(blk, m, 0, dp).wait_recv()
+    def send(m):
+        for s in range(1, hi):
+            copy_of(z, m, s).start()
 
     slot = (
         lax.broadcasted_iota(jnp.int32, seq_ref.shape, 0) * lanes
@@ -142,15 +128,17 @@
     for ch in range(CHUNKS):
         for c in load(ch):
             c.wait()
+        if ch + AHEAD < CHUNKS:
+            for c in load(ch + AHEAD):
+                c.start()
         at = pl.ds(ch * rows, rows)
         both = jnp.dot(xb[at], wide_in[...], preferred_element_type=jnp.float32)
         both += jnp.dot(gb[at], wide_out[...], preferred_element_type=jnp.float32)
         fac[z * CHUNKS + ch] = both.T[: 2 * rank].astype(jnp.bfloat16)
         if ch == 0:
-            greeted = (lo - 1) + (n_exp - 1) + jnp.where(z > 0, 1, 0) + jnp.where(z < hi - 1, 1, 0)
-            pl.semaphore_wait(barrier, greeted)
-            send_on(z, 0, start)
-        send_on(z, ch + 1, start)
+            pl.semaphore_wait(barrier, (lo - 1) + (n_exp - 1) + (hi - 1))
+            send(0)
+        send(ch + 1)
 
     def build(blk):
         for ch in range(CHUNKS):
@@ -194,31 +182,20 @@
             device_id_type=MESH,
         )
 
-    def receive(d):
-        for m in range(msgs):
-            for side in (-1, 1):
-                sz = z + side * d
-
-                @pl.when((sz >= 0) & (sz < hi))
-                def _():
-                    recv(sz, m)
-                    send_on(sz, m, start)
-
     for s in range(1, n_exp):
         log_copy(s).start()
     keep = pltpu.make_async_copy(rows_of(ex), logged_ref.at[ex], local_sem)
     keep.start()
-    receive(1)
     acc[...] = gram()
 
     def at_distance(d, carry):
-        receive(d + 1)
-
         def one(side, carry):
             sz = z + d * (2 * side - 1)
 
             @pl.when((sz >= 0) & (sz < hi))
             def _():
+                for m in range(msgs):
+                    copy_of(sz, m, 1).wait_recv()
                 build(sz)
                 acc[...] += gram()
 
@@ -278,12 +255,9 @@
                 :, c * lanes : (c + 1) * lanes
             ]
 
-    def drain(sz, carry):
+    for s in range(1, hi):
         for m in range(msgs):
-            send_on(sz, m, lambda c: c.wait_send())
-        return carry
-
-    lax.fori_loop(0, hi, drain, 0)
+            copy_of(z, m, s).wait_send()
     for s in range(1, lo):
         for q in range(-1, PIECES):
             across(s, q).wait_send()
@@ -293,36 +267,29 @@
 
 
 def place_kernel(pieces, *refs):
-    in_sems, out_sems = refs[-2:]
-    n = (len(refs) - 2) // 3
-    loads, stores = [], []
-    for src, dst, held in zip(refs[:n], refs[n : 2 * n], refs[2 * n : 3 * n]):
+    sems = refs[-1]
+    n = len(refs) // 2
+    stores = []
+    for src, dst in zip(refs[:n], refs[n:-1]):
         step = src.shape[0] // pieces
         for i in range(pieces):
             at = pl.ds(i * step, step)
-            k = len(loads)
-            loads.append(pltpu.make_async_copy(src.at[at], held.at[at], in_sems.at[k]))
-            stores.append(pltpu.make_async_copy(held.at[at], dst.at[at], out_sems.at[k]))
-    for c in loads:
+            stores.append(pltpu.make_async_copy(src.at[at], dst.at[at], sems.at[len(stores)]))
+    for c in stores:
         c.start()
-    for c, d in zip(loads, stores):
+    for c in stores:
         c.wait()
-        d.start()
-    for d in stores:
-        d.wait()
 
 
 def place(*arrays):
     pieces = 4
-    hbm = pl.BlockSpec(memory_space=pl.ANY)
     return pl.pallas_call(
         functools.partial(place_kernel, pieces),
         out_shape=tuple(jax.ShapeDtypeStruct(a.shape, a.dtype) for a in arrays),
-        in_specs=[hbm] * len(arrays),
-        out_specs=(hbm,) * len(arrays),
-        scratch_shapes=[pltpu.VMEM(a.shape, a.dtype) for a in arrays]
-        + [pltpu.SemaphoreType.DMA((pieces * len(arrays),))] * 2,
-        compiler_params=pltpu.CompilerParams(vmem_limit_bytes=60 * 1024 * 1024),
+        in_specs=[pl.BlockSpec(memory_space=pltpu.VMEM)] * len(arrays),
+        out_specs=(pl.BlockSpec(memory_space=pl.ANY),) * len(arrays),
+        scratch_shapes=[pltpu.SemaphoreType.DMA((pieces * len(arrays),))],
+        compiler_params=pltpu.CompilerParams(vmem_limit_bytes=4 * 1024 * 1024),
         name="place",
     )(*arrays)
 
@@ -343,8 +310,8 @@
     logged, fisher = pl.pallas_call(
         functools.partial(kernel, n_dp, n_exp, lo),
         out_shape=(
-            jax.ShapeDtypeStruct((n_exp, share, square), jnp.bfloat16),
-            jax.ShapeDtypeStruct((square // n_dp * square // lanes, lanes), jnp.float32),
+            pltpu.VMEM((n_exp, share, square), jnp.bfloat16),
+            pltpu.VMEM((square // n_dp * square // lanes, lanes), jnp.float32),
         ),
         in_specs=[pl.BlockSpec(memory_space=pltpu.SMEM), vmem, hbm, hbm, hbm, hbm],
         out_specs=(hbm, vmem),
@@ -367,7 +334,7 @@
             pltpu.VMEM((lo, cap // lanes, lanes), jnp.float32),
             pltpu.SemaphoreType.DMA((2 * CHUNKS,)),
             pltpu.SemaphoreType.DMA((2,)),
-            pltpu.SemaphoreType.DMA((2 * hi * msgs,)),
+            pltpu.SemaphoreType.DMA(((hi - 1) * msgs,)),
             pltpu.SemaphoreType.DMA((hi * msgs,)),
             pltpu.SemaphoreType.DMA((n_exp - 1,)),
             pltpu.SemaphoreType.DMA((n_exp - 1,)),

time: 35.8 us -> 33.5 us (0.936)
  Pallas kernels: 34.4 us -> 32 us
    pallas_call x1, Pallas kernels: 32.3 us -> 31 us  [body(): pl.pallas_call(functools.partial(kernel, n_dp, n_exp, lo), out_shape=(plt...]
    pallas_call x1, Pallas kernels: 2.09 us -> 1.03 us  [place(): pl.pallas_call(functools.partial(place_kernel, pieces), out_shape=tuple((...]
where the time goes in v1:
time: 33.5 us; the launch traced here: 33.3 us
  Pallas kernels  32 us (96%)
  between operations  1.28 us (4%)
    pallas_call x1, Pallas kernels, body(): pl.pallas_call(functools.partial(kernel, n_dp, n_exp, lo), out_shape=(plt...  31 us
    pallas_call x1, Pallas kernels, place(): pl.pallas_call(functools.partial(place_kernel, pieces), out_shape=tuple((...  1.03 us

profile of v1, /device:TPU:0, one launch (start us, length us, event | category | flops | bytes accessed | tf_op | source)
XLA Modules:
  0.0 33.3 jit_solution(12488783538764321379)
XLA Ops:
  1.3 31.0 %shard_map.77 = (bf16[4,64,1024]{2,1,0:T(8,128)(2,1)S(1)}, f32[1024,128]{1,0:T(8,128)S(1)}) custom-call(s32[1,1]{1,0:T(1,128)S(6)} %copy.9.count_ref, s32[8,128]{1,0:T(8,128)} %bitcast.10, bf16[1024,4096]{1,0:T(8,128)(2,1)} %bitcast.6, bf16[1024,1536]{1,0:T(8,128)(2,1)} %bitcast.7, bf16[32,4096]{1,0:T(8,128)(2,1)} %bitcast.8, bf16[32,1536]{1,0:T(8,128)(2,1)} %bitcast.9), custom_call_target="tpu_custom_call" | custom-call | tf_op jit(solution)/shard_map/pallas_call | solution.py:310
  32.2 1.0 %place.1 = (bf16[4,64,1024]{2,1,0:T(8,128)(2,1)}, f32[1024,128]{1,0:T(8,128)}) custom-call(bf16[4,64,1024]{2,1,0:T(8,128)(2,1)S(1)} %get-tuple-element.6.refs_0_, f32[1024,128]{1,0:T(8,128)S(1)} %get-tuple-element.7.refs_1_), custom_call_target="tpu_custom_call" | custom-call | tf_op jit(solution)/shard_map/place/pallas_call | solution.py:286

commit v2 on v1

--- a/solution.py
+++ b/solution.py
@@ -75,7 +75,7 @@
         c.start()
 
     def load(ch):
-        at = pl.ds(ch * rows, rows)
+        at = pl.ds(pl.multiple_of(ch * rows, rows), rows) if not isinstance(ch, int) else pl.ds(ch * rows, rows)
         return (
             pltpu.make_async_copy(x_hbm.at[at], xb.at[at], in_sem.at[2 * ch]),
             pltpu.make_async_copy(g_hbm.at[at], gb.at[at], in_sem.at[2 * ch + 1]),
@@ -99,7 +99,7 @@
         greet((lax.rem(z + s, hi) * lo + x, ex))
 
     def copy_of(src, m, s):
-        ref = seqs.at[src] if m == 0 else fac.at[src * CHUNKS + (m - 1)]
+        ref = seqs.at[src] if isinstance(m, int) and m == 0 else fac.at[src * CHUNKS + (m - 1)]
         return pltpu.make_async_remote_copy(
             src_ref=ref,
             dst_ref=ref,
@@ -121,24 +121,50 @@
 
     for c in p_copies:
         c.wait()
-    for src, dst, before in ((pin, wide_in, 0), (pout, wide_out, rank)):
-        blank = lambda r: [jnp.zeros((r, src.shape[1]), jnp.float32)] if r else []
-        tall = blank(before) + [src[...].astype(jnp.float32)] + blank(lanes - rank - before)
+    for src, dst in ((pin, wide_in), (pout, wide_out)):
+        depth = dst.shape[0]
+        groups = src.shape[1] // depth
+        tall = [src[:, i * depth : (i + 1) * depth].astype(jnp.float32) for i in range(groups)]
+        if groups * rank < lanes:
+            tall.append(jnp.zeros((lanes - groups * rank, depth), jnp.float32))
         dst[...] = jnp.concatenate(tall, axis=0).T.astype(jnp.bfloat16)
-    for ch in range(CHUNKS):
+
+    pl.semaphore_wait(barrier, (lo - 1) + (n_exp - 1) + (hi - 1))
+    send(0)
+    group = lax.broadcasted_iota(jnp.int32, (rows, lanes), 1) // rank
+
+    def project(buf, wide, at):
+        depth = wide.shape[0]
+        groups = buf.shape[1] // depth
+        total = jnp.zeros((rows, lanes), jnp.float32)
+        for i in range(groups):
+            part = jnp.dot(
+                buf[at, i * depth : (i + 1) * depth], wide[...], preferred_element_type=jnp.float32
+            )
+            total = jnp.where(group == i, part, total)
+        turned = total.T
+        out = turned[:rank]
+        for i in range(1, groups):
+            out += turned[i * rank : (i + 1) * rank]
+        return out.astype(jnp.bfloat16)
+
+    def chunk(ch, carry):
         for c in load(ch):
             c.wait()
-        if ch + AHEAD < CHUNKS:
+
+        @pl.when(ch + AHEAD < CHUNKS)
+        def _():
             for c in load(ch + AHEAD):
                 c.start()
-        at = pl.ds(ch * rows, rows)
-        both = jnp.dot(xb[at], wide_in[...], preferred_element_type=jnp.float32)
-        both += jnp.dot(gb[at], wide_out[...], preferred_element_type=jnp.float32)
-        fac[z * CHUNKS + ch] = both.T[: 2 * rank].astype(jnp.bfloat16)
-        if ch == 0:
-            pl.semaphore_wait(barrier, (lo - 1) + (n_exp - 1) + (hi - 1))
-            send(0)
+
+        at = pl.ds(pl.multiple_of(ch * rows, rows), rows)
+        mine = z * CHUNKS + ch
+        fac[mine, :rank] = project(xb, wide_in, at)
+        fac[mine, rank:] = project(gb, wide_out, at)
         send(ch + 1)
+        return carry
+
+    lax.fori_loop(0, CHUNKS, chunk, 0)
 
     def build(blk):
         for ch in range(CHUNKS):
@@ -163,11 +189,6 @@
         mine = gt[pl.ds(pl.multiple_of(z * lo * fb, lo * fb), lo * fb), :]
         return lax.dot_general(mine, gt[...], NT, preferred_element_type=jnp.float32)
 
-    build(z)
-    lg[...] = lax.dot_general(
-        onehot[...], outer[...], NT, preferred_element_type=jnp.float32
-    ).astype(jnp.bfloat16)
-
     def rows_of(e):
         return lg.at[pl.ds(pl.multiple_of(e * share, share), share)]
 
@@ -182,28 +203,36 @@
             device_id_type=MESH,
         )
 
-    for s in range(1, n_exp):
-        log_copy(s).start()
     keep = pltpu.make_async_copy(rows_of(ex), logged_ref.at[ex], local_sem)
-    keep.start()
-    acc[...] = gram()
-
-    def at_distance(d, carry):
-        def one(side, carry):
-            sz = z + d * (2 * side - 1)
-
-            @pl.when((sz >= 0) & (sz < hi))
+    acc[...] = jnp.zeros_like(acc)
+
+    def block(t, carry):
+        d = (t + 1) // 2
+        sz = z + d * (2 * lax.rem(t, 2) - 1)
+
+        @pl.when((sz >= 0) & (sz < hi))
+        def _():
+            @pl.when(t > 0)
             def _():
                 for m in range(msgs):
                     copy_of(sz, m, 1).wait_recv()
-                build(sz)
-                acc[...] += gram()
-
-            return carry
-
-        return lax.fori_loop(0, 2, one, carry)
-
-    lax.fori_loop(1, hi, at_distance, 0)
+
+            build(sz)
+
+            @pl.when(t == 0)
+            def _():
+                lg[...] = lax.dot_general(
+                    onehot[...], outer[...], NT, preferred_element_type=jnp.float32
+                ).astype(jnp.bfloat16)
+                for s in range(1, n_exp):
+                    log_copy(s).start()
+                keep.start()
+
+            acc[...] += gram()
+
+        return carry
+
+    lax.fori_loop(0, 2 * hi - 1, block, 0)
 
     live = jnp.zeros(seq_ref.shape, jnp.float32)
     for p in range(hi):
@@ -264,6 +293,13 @@
     keep.wait()
     for s in range(1, n_exp):
         log_copy(s).wait()
+
+
+def groups_of(depth, rank):
+    for groups in (4, 3, 2):
+        if groups * rank <= 128 and depth % (groups * 256) == 0:
+            return groups
+    return 1
 
 
 def place_kernel(pieces, *refs):
@@ -320,8 +356,8 @@
             pltpu.VMEM((cap, ff), jnp.bfloat16),
             pltpu.VMEM((rank, width), jnp.bfloat16),
             pltpu.VMEM((rank, ff), jnp.bfloat16),
-            pltpu.VMEM((width, lanes), jnp.bfloat16),
-            pltpu.VMEM((ff, lanes), jnp.bfloat16),
+            pltpu.VMEM((width // groups_of(width, rank), lanes), jnp.bfloat16),
+            pltpu.VMEM((ff // groups_of(ff, rank), lanes), jnp.bfloat16),
             pltpu.VMEM((hi * CHUNKS, 2 * rank, rows), jnp.bfloat16),
             pltpu.VMEM((hi, cap // lanes, lanes), jnp.int32),
             pltpu.VMEM((square, cap), jnp.bfloat16),

time: 33.5 us -> 33.7 us (level)
  no operation moved by 1% of the time
where the time goes in v2:
time: 33.7 us; the launch traced here: 33.5 us
  Pallas kernels  32.2 us (96%)
  between operations  1.28 us (4%)
    pallas_call x1, Pallas kernels, body(): pl.pallas_call(functools.partial(kernel, n_dp, n_exp, lo), out_shape=(plt...  31.2 us
    pallas_call x1, Pallas kernels, place(): pl.pallas_call(functools.partial(place_kernel, pieces), out_shape=tuple((...  1.03 us

profile of v2, /device:TPU:0, one launch (start us, length us, event | category | flops | bytes accessed | tf_op | source)
XLA Modules:
  0.0 33.5 jit_solution(18270226781138179728)
XLA Ops:
  1.3 31.2 %shard_map.77 = (bf16[4,64,1024]{2,1,0:T(8,128)(2,1)S(1)}, f32[1024,128]{1,0:T(8,128)S(1)}) custom-call(s32[1,1]{1,0:T(1,128)S(6)} %copy.9.count_ref, s32[8,128]{1,0:T(8,128)} %bitcast.10, bf16[1024,4096]{1,0:T(8,128)(2,1)} %bitcast.6, bf16[1024,1536]{1,0:T(8,128)(2,1)} %bitcast.7, bf16[32,4096]{1,0:T(8,128)(2,1)} %bitcast.8, bf16[32,1536]{1,0:T(8,128)(2,1)} %bitcast.9), custom_call_target="tpu_custom_call" | custom-call | tf_op jit(solution)/shard_map/pallas_call | solution.py:346
  32.5 1.0 %place.1 = (bf16[4,64,1024]{2,1,0:T(8,128)(2,1)}, f32[1024,128]{1,0:T(8,128)}) custom-call(bf16[4,64,1024]{2,1,0:T(8,128)(2,1)S(1)} %get-tuple-element.6.refs_0_, f32[1024,128]{1,0:T(8,128)S(1)} %get-tuple-element.7.refs_1_), custom_call_target="tpu_custom_call" | custom-call | tf_op jit(solution)/shard_map/place/pallas_call | solution.py:322

commit v3 on v2

--- a/solution.py
+++ b/solution.py
@@ -51,6 +51,8 @@
     lrecv_sem,
     xsend_sem,
     xrecv_sem,
+    fsend_sem,
+    frecv_sem,
     local_sem,
 ):
     hi = n_dp // lo
@@ -205,12 +207,15 @@
 
     keep = pltpu.make_async_copy(rows_of(ex), logged_ref.at[ex], local_sem)
     acc[...] = jnp.zeros_like(acc)
+    lives[0] = jnp.zeros(seq_ref.shape, jnp.float32)
+
+    far = jnp.where(2 * z < hi, hi - 1, 0)
 
     def block(t, carry):
         d = (t + 1) // 2
         sz = z + d * (2 * lax.rem(t, 2) - 1)
 
-        @pl.when((sz >= 0) & (sz < hi))
+        @pl.when((sz >= 0) & (sz < hi) & (sz != far))
         def _():
             @pl.when(t > 0)
             def _():
@@ -218,6 +223,7 @@
                     copy_of(sz, m, 1).wait_recv()
 
             build(sz)
+            lives[0] += jnp.where(seqs[sz] >= 0, 1.0, 0.0)
 
             @pl.when(t == 0)
             def _():
@@ -234,10 +240,7 @@
 
     lax.fori_loop(0, 2 * hi - 1, block, 0)
 
-    live = jnp.zeros(seq_ref.shape, jnp.float32)
-    for p in range(hi):
-        live += jnp.where(seqs[p] >= 0, 1.0, 0.0)
-    lives[0] = live
+    live = lives[0]
 
     piece = fb // PIECES
 
@@ -267,9 +270,37 @@
             at = pl.ds(pl.multiple_of(theirs + q * piece, piece), piece)
             give[s, rows_at(q)] = acc[at].astype(jnp.bfloat16)
             across(s, q).start()
+    def pass_on(s, m):
+        to = z * lo + lax.rem(x + s, lo)
+        spare = hi + s - 1
+        if m == 0:
+            src, dst = seqs.at[far], seqs.at[spare]
+        else:
+            src, dst = fac.at[far * CHUNKS + m - 1], fac.at[spare * CHUNKS + m - 1]
+        return pltpu.make_async_remote_copy(
+            src_ref=src,
+            dst_ref=dst,
+            send_sem=fsend_sem.at[(s - 1) * msgs + m],
+            recv_sem=frecv_sem.at[(s - 1) * msgs + m],
+            device_id=(to, ex),
+            device_id_type=MESH,
+        )
+
+    for m in range(msgs):
+        copy_of(far, m, 1).wait_recv()
+        for s in range(1, lo):
+            pass_on(s, m).start()
+
+    build(far)
+    acc[...] += gram()
+    live += jnp.where(seqs[far] >= 0, 1.0, 0.0)
     for s in range(1, lo):
+        for m in range(msgs):
+            pass_on(s, m).wait_recv()
+        build(hi + s - 1)
+        acc[...] += gram()
         across(s, -1).wait_recv()
-        live += lives[s]
+        live += lives[s] + jnp.where(seqs[hi + s - 1] >= 0, 1.0, 0.0)
     scale = 1.0 / jnp.sum(live)
     tiles = acc.shape[1] // lanes
     for q in range(PIECES):
@@ -290,6 +321,8 @@
     for s in range(1, lo):
         for q in range(-1, PIECES):
             across(s, q).wait_send()
+        for m in range(msgs):
+            pass_on(s, m).wait_send()
     keep.wait()
     for s in range(1, n_exp):
         log_copy(s).wait()
@@ -358,8 +391,8 @@
             pltpu.VMEM((rank, ff), jnp.bfloat16),
             pltpu.VMEM((width // groups_of(width, rank), lanes), jnp.bfloat16),
             pltpu.VMEM((ff // groups_of(ff, rank), lanes), jnp.bfloat16),
-            pltpu.VMEM((hi * CHUNKS, 2 * rank, rows), jnp.bfloat16),
-            pltpu.VMEM((hi, cap // lanes, lanes), jnp.int32),
+            pltpu.VMEM(((hi + lo - 1) * CHUNKS, 2 * rank, rows), jnp.bfloat16),
+            pltpu.VMEM((hi + lo - 1, cap // lanes, lanes), jnp.int32),
             pltpu.VMEM((square, cap), jnp.bfloat16),
             pltpu.VMEM((SEQ_DEV, cap), jnp.bfloat16),
             pltpu.VMEM((square, SEQ_DEV), jnp.bfloat16),
@@ -376,6 +409,8 @@
             pltpu.SemaphoreType.DMA((n_exp - 1,)),
             pltpu.SemaphoreType.DMA((max(lo - 1, 1) * (PIECES + 1),)),
             pltpu.SemaphoreType.DMA((max(lo - 1, 1) * (PIECES + 1),)),
+            pltpu.SemaphoreType.DMA((max(lo - 1, 1) * msgs,)),
+            pltpu.SemaphoreType.DMA((max(lo - 1, 1) * msgs,)),
             pltpu.SemaphoreType.DMA,
         ],
         compiler_params=pltpu.CompilerParams(

time: 33.7 us -> 36.8 us (1.092)
  Pallas kernels: 32.2 us -> 35.3 us
    pallas_call x1, Pallas kernels: 31.2 us -> 34.3 us  [body(): pl.pallas_call(functools.partial(kernel, n_dp, n_exp, lo), out_shape=(plt...]
where the time goes in v3:
time: 36.8 us; the launch traced here: 36.6 us
  Pallas kernels  35.3 us (96%)
  between operations  1.28 us (3%)
    pallas_call x1, Pallas kernels, body(): pl.pallas_call(functools.partial(kernel, n_dp, n_exp, lo), out_shape=(plt...  34.3 us
    pallas_call x1, Pallas kernels, place(): pl.pallas_call(functools.partial(place_kernel, pieces), out_shape=tuple((...  1.03 us

profile of v3, /device:TPU:0, one launch (start us, length us, event | category | flops | bytes accessed | tf_op | source)
XLA Modules:
  0.0 36.6 jit_solution(3906149667409358022)
XLA Ops:
  1.3 34.3 %shard_map.77 = (bf16[4,64,1024]{2,1,0:T(8,128)(2,1)S(1)}, f32[1024,128]{1,0:T(8,128)S(1)}) custom-call(s32[1,1]{1,0:T(1,128)S(6)} %copy.9.count_ref, s32[8,128]{1,0:T(8,128)} %bitcast.10, bf16[1024,4096]{1,0:T(8,128)(2,1)} %bitcast.6, bf16[1024,1536]{1,0:T(8,128)(2,1)} %bitcast.7, bf16[32,4096]{1,0:T(8,128)(2,1)} %bitcast.8, bf16[32,1536]{1,0:T(8,128)(2,1)} %bitcast.9), custom_call_target="tpu_custom_call" | custom-call | tf_op jit(solution)/shard_map/pallas_call | solution.py:379
  35.5 1.0 %place.1 = (bf16[4,64,1024]{2,1,0:T(8,128)(2,1)}, f32[1024,128]{1,0:T(8,128)}) custom-call(bf16[4,64,1024]{2,1,0:T(8,128)(2,1)S(1)} %get-tuple-element.6.refs_0_, f32[1024,128]{1,0:T(8,128)S(1)} %get-tuple-element.7.refs_1_), custom_call_target="tpu_custom_call" | custom-call | tf_op jit(solution)/shard_map/place/pallas_call | solution.py:355

commit v4 on v1

--- a/solution.py
+++ b/solution.py
@@ -144,11 +144,12 @@
         for ch in range(CHUNKS):
             at = pl.ds(ch * rows, rows)
             f = fac[blk * CHUNKS + ch]
-            wide = f[rank:].astype(jnp.float32)
+            wide = f.astype(jnp.float32)
+            low = wide[:rank]
             for k in range(rank):
-                row = jnp.broadcast_to(wide[k : k + 1], (16, rows)).astype(jnp.bfloat16)
-                for h in range(0, rank, 16):
-                    outer[k * rank + h : k * rank + h + 16, at] = row * f[h : h + 16]
+                outer[k * rank : (k + 1) * rank, at] = (wide[rank + k : rank + k + 1] * low).astype(
+                    jnp.bfloat16
+                )
         ids = seqs[blk]
         want = lax.broadcasted_iota(jnp.int32, (SEQ_DEV, lanes), 0)
         for c in range(cap // lanes):

time: 33.5 us -> 33.5 us (level)
  no operation moved by 1% of the time
where the time goes in v4:
time: 33.5 us; the launch traced here: 33.3 us
  Pallas kernels  32 us (96%)
  between operations  1.28 us (4%)
    pallas_call x1, Pallas kernels, body(): pl.pallas_call(functools.partial(kernel, n_dp, n_exp, lo), out_shape=(plt...  31 us
    pallas_call x1, Pallas kernels, place(): pl.pallas_call(functools.partial(place_kernel, pieces), out_shape=tuple((...  1.03 us

profile of v4, /device:TPU:0, one launch (start us, length us, event | category | flops | bytes accessed | tf_op | source)
XLA Modules:
  0.0 33.3 jit_solution(1908348765795117978)
XLA Ops:
  1.3 31.0 %shard_map.77 = (bf16[4,64,1024]{2,1,0:T(8,128)(2,1)S(1)}, f32[1024,128]{1,0:T(8,128)S(1)}) custom-call(s32[1,1]{1,0:T(1,128)S(6)} %copy.9.count_ref, s32[8,128]{1,0:T(8,128)} %bitcast.10, bf16[1024,4096]{1,0:T(8,128)(2,1)} %bitcast.6, bf16[1024,1536]{1,0:T(8,128)(2,1)} %bitcast.7, bf16[32,4096]{1,0:T(8,128)(2,1)} %bitcast.8, bf16[32,1536]{1,0:T(8,128)(2,1)} %bitcast.9), custom_call_target="tpu_custom_call" | custom-call | tf_op jit(solution)/shard_map/pallas_call | solution.py:311
  32.3 1.0 %place.1 = (bf16[4,64,1024]{2,1,0:T(8,128)(2,1)}, f32[1024,128]{1,0:T(8,128)}) custom-call(bf16[4,64,1024]{2,1,0:T(8,128)(2,1)S(1)} %get-tuple-element.6.refs_0_, f32[1024,128]{1,0:T(8,128)S(1)} %get-tuple-element.7.refs_1_), custom_call_target="tpu_custom_call" | custom-call | tf_op jit(solution)/shard_map/place/pallas_call | solution.py:287
